TPU v7x, 32 devices: a whole 2x2x4 slice. The times are simulated.
32 devices in a mesh: sec: 2 (over core), tile: 16 (over z, y, x).
Axes of the slice: x: 2, y: 2, z: 4, core: 2. Of those that a mesh axis runs over, the one named last changes fastest.
Arguments:
- adjoint_state: bfloat16 [2, 75, 589824], P('sec', None, 'tile'), may hold values from -6 to 6
- tangent_coef: bfloat16 [2, 75, 589824], P('sec', None, 'tile'), may hold values from 0.5 to 1.5
- column_ops: bfloat16 [2, 16, 75, 75], P('sec')
- surf_read: bfloat16 [2, 4, 75], P('sec'), may hold values from -0.75 to 0.75
- surf_write: float32 [2, 75, 4], P('sec'), may hold values from -3 to 3
- remap_weights: bfloat16 [16, 16, 16, 4096], P('tile')
- pair_atmos: int32 [16, 16, 16], P('tile'), may hold values from 0 to 575
- pair_ocean: int32 [16, 16, 16], P('tile'), may hold values from 0 to 9215, as said below
- list_len: int32 [16, 16], P('tile'), may hold values from 0 to 16, as said below
- ocean_owned: int32 [16, 576], P('tile'), may hold values from 0 to 9215, as said below
Outputs:
- adjoint_out: bfloat16 [2, 75, 589824], P('sec', None, 'tile')
Inputs may be any that keep to these rules, and one draw needn't show every extreme that they name: pair_ocean[t, d, c] is one of the blocks in row d of ocean_owned. Every global ocean block stands exactly once in ocean_owned. Slots c >= list_len[t, d] are empty; in every draw some ocean tile receives a full list of 16 pairs from every atmosphere tile.
All inputs are finite; a program needn't handle non-finite values.
Results may differ from a plain program's by a relative error of at most 0.012.
Values may be sent and summed in bfloat16 or wider, within the bound.
A program may use at most 128 MiB of HBM per device.

v0:
```python
import functools

import jax
import jax.numpy as jnp
from jax import lax
from jax.experimental import pallas as pl
from jax.experimental.pallas import tpu as pltpu
from jax.sharding import PartitionSpec as P

NF = 4
BLK = 64
MXU = 256
MESH = pl.DeviceIdType.MESH
F32 = jnp.float32
BF16 = jnp.bfloat16


def round_up(value, unit):
    return -(-value // unit) * unit


def iota(shape, axis):
    return lax.broadcasted_iota(jnp.int32, shape, axis)


def dot(left, right, contract=((1,), (0,))):
    return lax.dot_general(left, right, (contract, ((), ())), preferred_element_type=F32)


def one_hot(condition):
    return jnp.where(condition, 1.0, 0.0).astype(BF16)


def slot_column(rows, cap):
    spread = jnp.concatenate([jnp.broadcast_to(row, (cap, row.shape[1])) for row in rows], axis=0)
    chosen = iota(spread.shape, 1) == lax.rem(iota(spread.shape, 0), cap)
    return jnp.sum(jnp.where(chosen, spread.astype(F32), 0.0), axis=1, keepdims=True)


def exchange_kernel(
    tiles, cap, surface_ref, weights_ref, atmos_ref, ocean_ref, len_ref, owned_ref, out_ref,
    ids_send, ids_recv, data_send, data_recv, expanded, summed, sems,
):
    section = lax.axis_index("sec")
    me = lax.axis_index("tile")
    other = 1 - section
    slots = tiles * cap
    blocks = surface_ref.shape[1]
    chunks = weights_ref.shape[1] // MXU
    per_chunk = MXU // BLK
    ids_out, ids_in, data_out, data_in = [sems.at[i] for i in range(4)]

    def peer(i):
        return lax.rem(me + i, tiles)

    barrier = pltpu.get_barrier_semaphore()

    @pl.loop(0, tiles)
    def _(i):
        pl.semaphore_signal(barrier, inc=1, device_id=(other, peer(i)), device_id_type=MESH)

    pl.semaphore_wait(barrier, tiles)

    def send(source, target, send_sem, recv_sem):
        @pl.loop(0, tiles)
        def _(i):
            pltpu.make_async_remote_copy(
                src_ref=source.at[peer(i)],
                dst_ref=target.at[me],
                send_sem=send_sem,
                recv_sem=recv_sem,
                device_id=(other, peer(i)),
                device_id_type=MESH,
            ).start()

    def wait_all(buffer, sem):
        pltpu.make_async_copy(buffer, buffer, sem).wait()

    def surface_rows():
        return jnp.concatenate([surface_ref[n] for n in range(NF)], axis=1)

    def emit(forcing):
        for n in range(NF):
            out_ref[n] = forcing[:, n * BLK : (n + 1) * BLK]

    @pl.when(section == 0)
    def _():
        for d in range(tiles):
            ids_send[d, 0:1, 0:cap] = ocean_ref[d : d + 1, :]
        send(ids_send, ids_recv, ids_out, ids_in)
        source = slot_column([atmos_ref[d : d + 1, :] for d in range(tiles)], cap)
        spread = jnp.broadcast_to(len_ref[...], (slots, tiles))
        owner = iota((slots, tiles), 1) == iota((slots, tiles), 0) // cap
        length = jnp.sum(jnp.where(owner, spread.astype(F32), 0.0), axis=1, keepdims=True)
        live = lax.rem(iota((slots, 1), 0), cap).astype(F32) < length
        place = one_hot((iota((slots, blocks), 1).astype(F32) == source) & live)
        picked = dot(place, surface_rows()).astype(BF16)
        fields = [picked[:, n * BLK : (n + 1) * BLK] for n in range(NF)]
        summed[...] = jnp.zeros_like(summed)

        @pl.loop(0, chunks)
        def _(q):
            weights = weights_ref[:, pl.ds(pl.multiple_of(q * MXU, MXU), MXU)].astype(F32)
            widen = one_hot(iota((BLK, MXU), 0) == q * per_chunk + iota((BLK, MXU), 1) // BLK)
            for n in range(NF):
                summed[n] += dot(fields[n], widen) * weights

        flux = jnp.zeros((slots, MXU), F32)
        for n in range(NF):
            fold = one_hot(iota((MXU, MXU), 1) == n * BLK + lax.rem(iota((MXU, MXU), 0), BLK))
            flux += dot(summed[n].astype(BF16), fold)
        data_send[...] = flux.astype(BF16).reshape(tiles, cap, MXU)
        send(data_send, data_recv, data_out, data_in)

        wait_all(data_recv, data_in)
        echoes = data_recv[...].reshape(slots, MXU)
        for n in range(NF):
            repeat = one_hot(iota((MXU, MXU), 0) == n * BLK + lax.rem(iota((MXU, MXU), 1), BLK))
            expanded[n] = dot(echoes, repeat)
        summed[:, :, 0:BLK] = jnp.zeros((NF, slots, BLK), F32)

        @pl.loop(0, chunks)
        def _(q):
            weights = weights_ref[:, pl.ds(pl.multiple_of(q * MXU, MXU), MXU)].astype(F32)
            gather = one_hot(iota((MXU, BLK), 1) == q * per_chunk + iota((MXU, BLK), 0) // BLK)
            for n in range(NF):
                summed[n, :, 0:BLK] += dot((expanded[n] * weights).astype(BF16), gather)

        back = jnp.concatenate([summed[n, :, 0:BLK] for n in range(NF)], axis=1)
        high = back.astype(BF16)
        low = (back - high.astype(F32)).astype(BF16)
        emit(dot(place, high, ((0,), (0,))) + dot(place, low, ((0,), (0,))))
        wait_all(ids_send, ids_out)
        wait_all(data_send, data_out)

    @pl.when(section == 1)
    def _():
        rows = surface_rows()
        wait_all(ids_recv, ids_in)
        wanted = slot_column([ids_recv[t, 0:1, :] for t in range(tiles)], cap)
        place = one_hot(owned_ref[...].astype(F32) == wanted)
        data_send[...] = dot(place, rows).astype(BF16).reshape(tiles, cap, MXU)
        send(data_send, data_recv, data_out, data_in)
        wait_all(data_recv, data_in)
        emit(dot(place, data_recv[...].reshape(slots, MXU), ((0,), (0,))))
        wait_all(data_send, data_out)


def exchange(surface, weights, pair_atmos, pair_ocean, list_len, owned):
    tiles, cap = pair_atmos.shape
    blocks = owned.shape[1]
    slots = tiles * cap
    return pl.pallas_call(
        functools.partial(exchange_kernel, tiles, cap),
        out_shape=jax.ShapeDtypeStruct((NF, blocks, BLK), F32),
        in_specs=[pl.BlockSpec(memory_space=pltpu.VMEM)] * 6,
        out_specs=pl.BlockSpec(memory_space=pltpu.VMEM),
        scratch_shapes=[
            pltpu.VMEM((tiles, 8, 128), jnp.int32),
            pltpu.VMEM((tiles, 8, 128), jnp.int32),
            pltpu.VMEM((tiles, cap, MXU), BF16),
            pltpu.VMEM((tiles, cap, MXU), BF16),
            pltpu.VMEM((NF, slots, MXU), F32),
            pltpu.VMEM((NF, slots, MXU), F32),
            pltpu.SemaphoreType.DMA((4,)),
        ],
        compiler_params=pltpu.CompilerParams(
            collective_id=0, has_side_effects=True, vmem_limit_bytes=48 * 1024 * 1024
        ),
        name="exchange",
    )(surface, weights, pair_atmos, pair_ocean, list_len, owned)


def sweep_kernel(levels, rows, group, lanes, units, state_ref, coef_ref, ops_ref, write_ref, forcing_ref, out_ref, big):
    steps = ops_ref.shape[0]
    full = big.shape[1]

    @pl.when(pl.program_id(0) == 0)
    def _():
        tiler = one_hot(
            (lax.rem(iota((rows, full), 1), rows) == iota((rows, full), 0)) & (iota((rows, full), 1) < group * rows)
        )
        lane = iota((rows, full), 1)
        for step in range(steps):
            tiled = dot(ops_ref[step], tiler)
            for part in range(group):
                inside = (lane >= part * rows) & (lane < (part + 1) * rows)
                big[step, part * rows : (part + 1) * rows, :] = jnp.where(inside, tiled, 0.0).astype(BF16)
            if full > group * rows:
                big[step, group * rows :, :] = jnp.zeros((full - group * rows, full), BF16)

    valid = iota((rows, lanes), 0) < levels

    def columns(unit, part):
        return pl.ds((unit * group + part) * lanes, lanes)

    def stacked(ref, unit):
        pieces = [jnp.where(valid, ref[0, :, columns(unit, part)].astype(F32), 0.0) for part in range(group)]
        if full > group * rows:
            pieces.append(jnp.zeros((full - group * rows, lanes), F32))
        return jnp.concatenate(pieces, axis=0).T

    current = [stacked(state_ref, unit).astype(BF16) for unit in range(units)]
    factors = [stacked(coef_ref, unit) for unit in range(units)]
    for step in range(steps):
        for unit in range(units):
            current[unit] = (dot(current[unit], big[step]) * factors[unit]).astype(BF16)

    write = write_ref[...]
    write_high = write.astype(BF16).astype(F32)
    write_parts = jnp.concatenate([write_high, write_high, write - write_high], axis=1).astype(BF16)
    for unit in range(units):
        swept = current[unit].astype(F32).T
        for part in range(group):
            forcing = forcing_ref[:, columns(unit, part)]
            high = forcing.astype(BF16).astype(F32)
            parts = jnp.concatenate([high, forcing - high, high], axis=0).astype(BF16)
            out_ref[0, :, columns(unit, part)] = (
                swept[part * rows : (part + 1) * rows] + dot(write_parts, parts)
            ).astype(BF16)


def sweep(state, coef, column_ops, surf_write, forcing):
    _, levels, cells = state.shape
    steps = column_ops.shape[1]
    rows = round_up(levels, 16)
    full = round_up(rows, MXU)
    group = full // rows
    lanes, units = next(
        (lanes, units)
        for lanes, units in ((512, 2), (512, 1), (256, 1), (128, 1))
        if cells % (group * lanes * units) == 0
    )
    block = group * lanes * units
    operators = jnp.pad(column_ops[0], ((0, 0), (0, rows - levels), (0, rows - levels)))
    write = jnp.pad(surf_write[0], ((0, rows - levels), (0, 0)))
    wide = pl.BlockSpec((1, rows, block), lambda i: (0, 0, i))
    return pl.pallas_call(
        functools.partial(sweep_kernel, levels, rows, group, lanes, units),
        out_shape=jax.ShapeDtypeStruct(state.shape, BF16),
        grid=(cells // block,),
        in_specs=[
            wide,
            wide,
            pl.BlockSpec(operators.shape, lambda i: (0, 0, 0)),
            pl.BlockSpec(write.shape, lambda i: (0, 0)),
            pl.BlockSpec((NF, block), lambda i: (0, i)),
        ],
        out_specs=wide,
        scratch_shapes=[pltpu.VMEM((steps, full, full), BF16)],
        compiler_params=pltpu.CompilerParams(
            dimension_semantics=("arbitrary",), vmem_limit_bytes=56 * 1024 * 1024
        ),
        name="sweep",
    )(state, coef, operators, write, forcing)


def body(
    adjoint_state,
    tangent_coef,
    column_ops,
    surf_read,
    surf_write,
    remap_weights,
    pair_atmos,
    pair_ocean,
    list_len,
    ocean_owned,
):
    tiles, cap = pair_atmos.shape[1:]
    blocks = ocean_owned.shape[1]
    surface = jnp.dot(surf_read[0], adjoint_state[0], preferred_element_type=F32).astype(BF16)
    forcing = exchange(
        surface.reshape(NF, blocks, BLK),
        remap_weights.reshape(tiles * cap, BLK * BLK),
        pair_atmos[0],
        pair_ocean[0],
        list_len,
        ocean_owned,
    )
    return sweep(adjoint_state, tangent_coef, column_ops, surf_write, forcing.reshape(NF, blocks * BLK))


def solution(mesh):
    in_specs = (
        P("sec", None, "tile"),
        P("sec", None, "tile"),
        P("sec", None, None, None),
        P("sec", None, None),
        P("sec", None, None),
        P("tile", None, None, None),
        P("tile", None, None),
        P("tile", None, None),
        P("tile", None),
        P("tile", None),
    )
    out_specs = P("sec", None, "tile")
    return jax.shard_map(body, mesh=mesh, in_specs=in_specs, out_specs=out_specs, check_vma=False)
```

profile of v0, /device:TPU:0, one launch (start us, length us, event | category | flops | bytes accessed | tf_op | source)
XLA Modules:
  0.0 64.3 jit_solution(10868210613422975806)
XLA Ops:
  0.0 0.0 copy-start
  0.0 0.0 copy-start.4
  0.0 0.0 copy-start.5
  0.0 0.0 copy-start.3
  0.0 0.0 copy-start.2
  0.0 0.0 copy-start.6
  0.0 0.8 %copy.14 = f32[1,75,4]{2,1,0:T(8,128)S(1)} copy(f32[1,75,4]{1,2,0:T(4,128)} %param.14) | data formatting | bytes 2400 | tf_op args[4]
  0.9 0.6 pad.9.write_ref
  1.5 0.0 copy-done
  1.5 3.5 %convolution_convert_fusion = bf16[4,36864]{1,0:T(4,128)(2,1)S(1)} fusion(bf16[1,75,36864]{2,1,0:T(8,128)(2,1)} %state_ref.1, bf16[1,4,75]{2,1,0:T(4,128)(2,1)S(1)} %copy-done), kind=kOutput, calls=%fused_computation | convolution fusion | flops 22265856 | bytes 5825112 | tf_op jit(solution)/shard_map/dot_general | solution.py:272
  5.0 0.5 reshape.9.surface_ref
  5.5 0.0 copy-done.6
  5.5 0.1 copy.16
  5.6 0.8 %pad.8.ops_ref = bf16[16,80,80]{2,1,0:T(8,128)(2,1)} pad(bf16[16,75,75]{2,1,0:T(8,128)(2,1)S(1)} %bitcast.16, bf16[]{:T(256)} %constant.3.clone.1), padding=0_0x0_5x0_5 | pad | bytes 384802 | tf_op jit(solution)/shard_map/jit(_pad)/pad | solution.py:235
  6.5 0.0 copy-done.4
  6.5 0.0 copy-done.5
  6.5 0.0 copy-done.3
  6.5 0.0 copy-done.2
  6.5 0.0 copy-start.1
  6.5 1.6 %copy-done.1 = bf16[1,16,16,4096]{3,2,1,0:T(8,128)(2,1)S(1)} copy-done((bf16[1,16,16,4096]{3,2,1,0:T(8,128)(2,1)S(1)}, bf16[1,16,16,4096]{3,2,1,0:T(8,128)(2,1)}, u32[]{:S(2)}) %copy-start.1) | copy-done | bytes 2097176
  8.1 21.3 %exchange.1 = f32[4,576,64]{2,1,0:T(8,128)S(1)} custom-call(bf16[4,576,64]{2,1,0:T(8,128)(2,1)S(1)} %reshape.9.surface_ref, bf16[256,4096]{1,0:T(8,128)(2,1)S(1)} %bitcast.13, s32[16,16]{1,0:T(8,128)S(1)} %bitcast.14, s32[16,16]{1,0:T(8,128)S(1)} %bitcast.15, s32[1,16]{1,0:T(1,128)S(1)} %copy-done.5, s32[1,576]{1,0:T(1,128)S(1)} %copy-done.4), custom_call_target="tpu_custom_call" | custom-call | tf_op jit(solution)/shard_map/exchange/pallas_call | solution.py:153
  29.4 1.3 %reshape.11.forcing_ref = f32[4,36864]{1,0:T(4,128)} reshape(f32[4,576,64]{2,1,0:T(8,128)S(1)} %exchange.1) | data formatting | bytes 1179648 | tf_op jit(solution)/shard_map/reshape | solution.py:281
  30.7 33.6 %sweep.1 = bf16[1,75,36864]{2,1,0:T(8,128)(2,1)} custom-call(bf16[1,75,36864]{2,1,0:T(8,128)(2,1)} %state_ref.1, bf16[1,75,36864]{2,1,0:T(8,128)(2,1)} %coef_ref.1, bf16[16,80,80]{2,1,0:T(8,128)(2,1)} %pad.8.ops_ref, f32[80,4]{1,0:T(8,128)} %pad.9.write_ref, f32[4,36864]{1,0:T(4,128)} %reshape.11.forcing_ref), custom_call_target="tpu_custom_call" | custom-call | tf_op jit(solution)/shard_map/sweep/pallas_call | solution.py:238
Async XLA Ops:
  0.0 1.5 %copy-start = (bf16[1,4,75]{2,1,0:T(4,128)(2,1)S(1)}, bf16[1,4,75]{2,1,0:T(4,128)(2,1)}, u32[]{:S(2)}) copy-start(bf16[1,4,75]{2,1,0:T(4,128)(2,1)} %param.13) | copy-start | bytes 1804
  0.0 6.5 %copy-start.4 = (s32[1,576]{1,0:T(1,128)S(1)}, s32[1,576]{1,0:T(1,128)}, u32[]{:S(2)}) copy-start(s32[1,576]{1,0:T(1,128)} %owned_ref.1) | copy-start | bytes 6916
  0.0 6.5 %copy-start.5 = (s32[1,16]{1,0:T(1,128)S(1)}, s32[1,16]{1,0:T(1,128)}, u32[]{:S(2)}) copy-start(s32[1,16]{1,0:T(1,128)} %len_ref.1) | copy-start | bytes 196
  0.0 6.5 %copy-start.3 = (s32[1,16,16]{2,1,0:T(8,128)S(1)}, s32[1,16,16]{2,1,0:T(8,128)}, u32[]{:S(2)}) copy-start(s32[1,16,16]{2,1,0:T(8,128)} %param.17) | copy-start | bytes 3076
  0.0 6.5 %copy-start.2 = (s32[1,16,16]{2,1,0:T(8,128)S(1)}, s32[1,16,16]{2,1,0:T(8,128)}, u32[]{:S(2)}) copy-start(s32[1,16,16]{2,1,0:T(8,128)} %param.16) | copy-start | bytes 3076
  0.0 5.5 %copy-start.6 = (bf16[1,16,75,75]{3,1,2,0:T(8,128)(2,1)S(1)}, bf16[1,16,75,75]{3,1,2,0:T(8,128)(2,1)}, u32[]{:S(2)}) copy-start(bf16[1,16,75,75]{3,1,2,0:T(8,128)(2,1)} %param.12) | copy-start | bytes 540004
  6.5 1.6 %copy-start.1 = (bf16[1,16,16,4096]{3,2,1,0:T(8,128)(2,1)S(1)}, bf16[1,16,16,4096]{3,2,1,0:T(8,128)(2,1)}, u32[]{:S(2)}) copy-start(bf16[1,16,16,4096]{3,2,1,0:T(8,128)(2,1)} %param.15) | copy-start | bytes 6291460
where the time goes:
time: 64.5 us; the launch traced here: 64.3 us
  Pallas kernels  54.9 us (85%)
  local copies, waits for them, and re-layouts  5.77 us (9%)
  matrix products  3.55 us (6%)
    pallas_call x1, Pallas kernels, sweep(): pl.pallas_call(functools.partial(sweep_kernel, levels, rows, group, lanes...  33.6 us
    pallas_call x1, Pallas kernels, exchange(): pl.pallas_call(functools.partial(exchange_kernel, tiles, cap), out_shape=...  21.3 us
    dot_general x1, matrix products, body(): jnp.dot(surf_read[0], adjoint_state[0], preferred_element_type=F32)  3.55 us
    unnamed x16, local copies, waits for them, and re-layouts  2.54 us
    reshape x1, local copies, waits for them, and re-layouts, body(): forcing.reshape(NF, blocks * BLK)  1.31 us

commit v1 on v0

v1 whole, which is shorter than its diff:
```python
import functools

import jax
import jax.numpy as jnp
from jax import lax
from jax.experimental import pallas as pl
from jax.experimental.pallas import tpu as pltpu
from jax.sharding import PartitionSpec as P

NF = 4
BLK = 64
MXU = 256
MESH = pl.DeviceIdType.MESH
F32 = jnp.float32
BF16 = jnp.bfloat16


def round_up(value, unit):
    return -(-value // unit) * unit


def iota(shape, axis):
    return lax.broadcasted_iota(jnp.int32, shape, axis)


def dot(left, right, contract=((1,), (0,))):
    return lax.dot_general(left, right, (contract, ((), ())), preferred_element_type=F32)


def one_hot(condition):
    return jnp.where(condition, 1.0, 0.0).astype(BF16)


def slot_column(rows, cap):
    spread = jnp.concatenate([jnp.broadcast_to(row, (cap, row.shape[1])) for row in rows], axis=0)
    chosen = iota(spread.shape, 1) == lax.rem(iota(spread.shape, 0), cap)
    return jnp.sum(jnp.where(chosen, spread.astype(F32), 0.0), axis=1, keepdims=True)


def exchange_kernel(
    tiles, cap, surface_ref, weights_ref, atmos_ref, ocean_ref, len_ref, owned_ref, out_ref,
    ids_send, ids_recv, flux_send, flux_recv, reply_send, reply_recv, back_half, back_recv,
    expanded, summed, folded, sems,
):
    section = lax.axis_index("sec")
    me = lax.axis_index("tile")
    other = 1 - section
    slots = tiles * cap
    half = tiles // 2
    half_slots = half * cap
    pairs = surface_ref.shape[1]
    blocks = 2 * pairs
    wide = 2 * MXU
    chunks = weights_ref.shape[1] // wide
    per_chunk = wide // BLK
    ids_out, ids_in, flux_out, flux_in, reply_out, reply_in, back_out, back_in = [sems.at[i] for i in range(8)]

    def peer(i):
        return lax.rem(me + i, tiles)

    barrier = pltpu.get_barrier_semaphore()

    @pl.loop(0, tiles)
    def _(i):
        pl.semaphore_signal(barrier, inc=1, device_id=(other, peer(i)), device_id_type=MESH)

    @pl.when(section == 1)
    def _():
        @pl.loop(1, tiles)
        def _(i):
            pl.semaphore_signal(barrier, inc=1, device_id=(section, peer(i)), device_id_type=MESH)

        pl.semaphore_wait(barrier, 2 * tiles - 1)

    @pl.when(section == 0)
    def _():
        pl.semaphore_wait(barrier, tiles)

    def send(source, target, send_sem, recv_sem, first, to):
        @pl.loop(first, tiles)
        def _(i):
            pltpu.make_async_remote_copy(
                src_ref=source.at[peer(i)],
                dst_ref=target,
                send_sem=send_sem,
                recv_sem=recv_sem,
                device_id=(to, peer(i)),
                device_id_type=MESH,
            ).start()

    def wait_all(buffer, sem):
        pltpu.make_async_copy(buffer, buffer, sem).wait()

    def surface_rows():
        lower = [surface_ref[n, :, 0:BLK] for n in range(NF)]
        upper = [surface_ref[n, :, BLK : 2 * BLK] for n in range(NF)]
        return jnp.concatenate([jnp.concatenate(lower, axis=1), jnp.concatenate(upper, axis=1)], axis=0)

    def emit(forcing):
        for n in range(NF):
            lanes = slice(n * BLK, (n + 1) * BLK)
            out_ref[n] = jnp.concatenate([forcing[:pairs, lanes], forcing[pairs:, lanes]], axis=1)

    def weights_at(q, first, count):
        return weights_ref[first : first + count, pl.ds(pl.multiple_of(q * wide, wide), wide)].astype(F32)

    def back_terms(first):
        echoes = reply_recv[...].reshape(half_slots, MXU)
        for n in range(NF):
            repeat = one_hot(iota((MXU, MXU), 0) == n * BLK + lax.rem(iota((MXU, MXU), 1), BLK))
            expanded[n] = dot(echoes, repeat)
        folded[...] = jnp.zeros_like(folded)

        @pl.loop(0, chunks)
        def _(q):
            weights = weights_at(q, first, half_slots)
            gather = one_hot(iota((wide, BLK), 1) == q * per_chunk + iota((wide, BLK), 0) // BLK)
            for n in range(NF):
                copies = jnp.concatenate([expanded[n], expanded[n]], axis=1)
                folded[n] += dot((copies * weights).astype(BF16), gather)

        back_half[...] = jnp.concatenate([folded[n] for n in range(NF)], axis=1).astype(BF16)

    @pl.when(section == 0)
    def _():
        for d in range(tiles):
            ids_send[d, 0:1, 0:cap] = ocean_ref[d : d + 1, :]
        send(ids_send, ids_recv.at[me], ids_out, ids_in, 0, 1)
        source = slot_column([atmos_ref[d : d + 1, :] for d in range(tiles)], cap)
        spread = jnp.broadcast_to(len_ref[...], (slots, tiles))
        owner = iota((slots, tiles), 1) == iota((slots, tiles), 0) // cap
        length = jnp.sum(jnp.where(owner, spread.astype(F32), 0.0), axis=1, keepdims=True)
        live = lax.rem(iota((slots, 1), 0), cap).astype(F32) < length
        lane = iota((slots, blocks), 1)
        block = 2 * lax.rem(lane, pairs) + lane // pairs
        place = one_hot((block.astype(F32) == source) & live)
        picked = dot(place, surface_rows()).astype(BF16)
        fields = [picked[:, n * BLK : (n + 1) * BLK] for n in range(NF)]
        summed[...] = jnp.zeros_like(summed)

        @pl.loop(0, chunks)
        def _(q):
            weights = weights_at(q, 0, slots)
            widen = one_hot(iota((BLK, wide), 0) == q * per_chunk + iota((BLK, wide), 1) // BLK)
            for n in range(NF):
                terms = dot(fields[n], widen) * weights
                summed[n] += terms[:, :MXU] + terms[:, MXU:]

        flux = jnp.zeros((slots, MXU), F32)
        for n in range(NF):
            fold = one_hot(iota((MXU, MXU), 1) == n * BLK + lax.rem(iota((MXU, MXU), 0), BLK))
            flux += dot(summed[n].astype(BF16), fold)
        flux_send[...] = flux.astype(BF16).reshape(tiles, cap, MXU)
        send(flux_send, flux_recv.at[me], flux_out, flux_in, 0, 1)

        wait_all(reply_recv, reply_in)
        back_terms(0)
        wait_all(back_recv, back_in)
        back = jnp.concatenate([back_half[...], back_recv[...]], axis=0)
        emit(dot(place, back, ((0,), (0,))))
        wait_all(ids_send, ids_out)
        wait_all(flux_send, flux_out)

    @pl.when(section == 1)
    def _():
        rows = surface_rows()
        wait_all(ids_recv, ids_in)
        wanted = slot_column([ids_recv[t, 0:1, :] for t in range(tiles)], cap)
        place = one_hot(owned_ref[...].astype(F32) == wanted)
        reply_send[...] = dot(place, rows).astype(BF16).reshape(tiles, cap, MXU)
        upper = me >= half

        @pl.when(upper)
        def _():
            send(reply_send, reply_recv.at[me - half], reply_out, reply_in, 1, 1)
            reply_recv[me - half] = reply_send[me]
            wait_all(reply_recv.at[pl.ds(0, half - 1)], reply_in)

        @pl.when(jnp.logical_not(upper))
        def _():
            send(reply_send, reply_recv.at[me], reply_out, reply_in, 0, 0)
            wait_all(reply_recv, reply_in)

        back_terms(half_slots)
        back_copy = pltpu.make_async_remote_copy(
            src_ref=back_half,
            dst_ref=back_recv,
            send_sem=back_out,
            recv_sem=back_in,
            device_id=(other, me),
            device_id_type=MESH,
        )
        back_copy.start()
        wait_all(flux_recv, flux_in)
        emit(dot(place, flux_recv[...].reshape(slots, MXU), ((0,), (0,))))
        back_copy.wait_send()

        @pl.when(upper)
        def _():
            wait_all(reply_send.at[pl.ds(0, tiles - 1)], reply_out)

        @pl.when(jnp.logical_not(upper))
        def _():
            wait_all(reply_send, reply_out)


def exchange(surface, weights, pair_atmos, pair_ocean, list_len, owned):
    tiles, cap = pair_atmos.shape
    pairs = surface.shape[1]
    slots = tiles * cap
    half = tiles // 2
    return pl.pallas_call(
        functools.partial(exchange_kernel, tiles, cap),
        out_shape=jax.ShapeDtypeStruct((NF, pairs, 2 * BLK), F32),
        in_specs=[pl.BlockSpec(memory_space=pltpu.VMEM)] * 6,
        out_specs=pl.BlockSpec(memory_space=pltpu.VMEM),
        scratch_shapes=[
            pltpu.VMEM((tiles, 8, 128), jnp.int32),
            pltpu.VMEM((tiles, 8, 128), jnp.int32),
            pltpu.VMEM((tiles, cap, MXU), BF16),
            pltpu.VMEM((tiles, cap, MXU), BF16),
            pltpu.VMEM((tiles, cap, MXU), BF16),
            pltpu.VMEM((half, cap, MXU), BF16),
            pltpu.VMEM((half * cap, MXU), BF16),
            pltpu.VMEM((half * cap, MXU), BF16),
            pltpu.VMEM((NF, half * cap, MXU), F32),
            pltpu.VMEM((NF, slots, MXU), F32),
            pltpu.VMEM((NF, half * cap, BLK), F32),
            pltpu.SemaphoreType.DMA((8,)),
        ],
        compiler_params=pltpu.CompilerParams(
            collective_id=0, has_side_effects=True, vmem_limit_bytes=48 * 1024 * 1024
        ),
        name="exchange",
    )(surface, weights, pair_atmos, pair_ocean, list_len, owned)


def sweep_kernel(levels, rows, group, lanes, units, state_ref, coef_ref, ops_ref, write_ref, forcing_ref, out_ref, big):
    steps = ops_ref.shape[0]
    full = big.shape[1]

    @pl.when(pl.program_id(0) == 0)
    def _():
        tiler = one_hot(
            (lax.rem(iota((levels, full), 1), rows) == iota((levels, full), 0))
            & (iota((levels, full), 1) < group * rows)
        )
        valid = iota((rows, levels), 0) < levels
        lane = iota((rows, full), 1)
        for step in range(steps):
            operator = jnp.where(valid, ops_ref[step].astype(F32), 0.0).astype(BF16)
            tiled = dot(operator, tiler)
            for part in range(group):
                inside = (lane >= part * rows) & (lane < (part + 1) * rows)
                big[step, part * rows : (part + 1) * rows, :] = jnp.where(inside, tiled, 0.0).astype(BF16)
            if full > group * rows:
                big[step, group * rows :, :] = jnp.zeros((full - group * rows, full), BF16)

    valid = iota((rows, lanes), 0) < levels

    def columns(unit, part):
        return pl.ds((unit * group + part) * lanes, lanes)

    def stacked(ref, unit):
        pieces = [
            jnp.where(valid, ref[0, :, columns(unit, part)].astype(F32), 0.0).astype(BF16) for part in range(group)
        ]
        if full > group * rows:
            pieces.append(jnp.zeros((full - group * rows, lanes), BF16))
        return jnp.concatenate(pieces, axis=0).T

    current = [stacked(state_ref, unit) for unit in range(units)]
    factors = [stacked(coef_ref, unit).astype(F32) for unit in range(units)]
    for step in range(steps):
        for unit in range(units):
            current[unit] = (dot(current[unit], big[step]) * factors[unit]).astype(BF16)

    write = write_ref[:, 0:rows]
    write_high = write.astype(BF16).astype(F32)
    write_parts = jnp.concatenate([write_high, write_high, write - write_high], axis=0).astype(BF16)
    for unit in range(units):
        swept = current[unit].T.astype(F32)
        for part in range(group):
            forcing = forcing_ref[:, columns(unit, part)]
            high = forcing.astype(BF16).astype(F32)
            parts = jnp.concatenate([high, forcing - high, high], axis=0).astype(BF16)
            out_ref[0, :, columns(unit, part)] = (
                swept[part * rows : (part + 1) * rows] + dot(write_parts, parts, ((0,), (0,)))
            ).astype(BF16)


def sweep(state, coef, column_ops, surf_write, forcing):
    _, levels, cells = state.shape
    steps = column_ops.shape[1]
    rows = round_up(levels, 16)
    full = round_up(rows, MXU)
    group = full // rows
    lanes, units = next(
        (lanes, units)
        for lanes, units in ((1024, 2), (512, 2), (512, 1), (256, 1), (128, 1))
        if cells % (group * lanes * units) == 0
    )
    block = group * lanes * units
    operators = column_ops[0]
    write = surf_write[0].T
    wide = pl.BlockSpec((1, rows, block), lambda i: (0, 0, i))
    return pl.pallas_call(
        functools.partial(sweep_kernel, levels, rows, group, lanes, units),
        out_shape=jax.ShapeDtypeStruct(state.shape, BF16),
        grid=(cells // block,),
        in_specs=[
            wide,
            wide,
            pl.BlockSpec((steps, rows, levels), lambda i: (0, 0, 0)),
            pl.BlockSpec((NF, round_up(rows, 128)), lambda i: (0, 0)),
            pl.BlockSpec((NF, block), lambda i: (0, i)),
        ],
        out_specs=wide,
        scratch_shapes=[pltpu.VMEM((steps, full, full), BF16)],
        compiler_params=pltpu.CompilerParams(
            dimension_semantics=("arbitrary",), vmem_limit_bytes=56 * 1024 * 1024
        ),
        name="sweep",
    )(state, coef, operators, write, forcing)


def body(
    adjoint_state,
    tangent_coef,
    column_ops,
    surf_read,
    surf_write,
    remap_weights,
    pair_atmos,
    pair_ocean,
    list_len,
    ocean_owned,
):
    tiles, cap = pair_atmos.shape[1:]
    pairs = ocean_owned.shape[1] // 2
    surface = jnp.dot(surf_read[0], adjoint_state[0], preferred_element_type=F32).astype(BF16)
    owned = jnp.swapaxes(ocean_owned.reshape(pairs, 2), 0, 1).reshape(1, 2 * pairs)
    forcing = exchange(
        surface.reshape(NF, pairs, 2 * BLK),
        remap_weights.reshape(tiles * cap, BLK * BLK),
        pair_atmos[0],
        pair_ocean[0],
        list_len,
        owned,
    )
    return sweep(adjoint_state, tangent_coef, column_ops, surf_write, forcing.reshape(NF, 2 * pairs * BLK))


def solution(mesh):
    in_specs = (
        P("sec", None, "tile"),
        P("sec", None, "tile"),
        P("sec", None, None, None),
        P("sec", None, None),
        P("sec", None, None),
        P("tile", None, None, None),
        P("tile", None, None),
        P("tile", None, None),
        P("tile", None),
        P("tile", None),
    )
    out_specs = P("sec", None, "tile")
    return jax.shard_map(body, mesh=mesh, in_specs=in_specs, out_specs=out_specs, check_vma=False)
```

time: 64.5 us -> 59.8 us (0.927)
  local copies, waits for them, and re-layouts: 5.77 us -> 2.39 us
  Pallas kernels: 54.9 us -> 52.7 us
  other arithmetic: 0 us -> 0.85 us
    pallas_call x1, Pallas kernels: 21.3 us -> 19.4 us  [exchange(): pl.pallas_call(functools.partial(exchange_kernel, tiles, cap), out_shape=...]
    reshape x2, local copies, waits for them, and re-layouts: 1.8 us -> 0.23 us  [the longest x1 0.14 us: body(): ocean_owned.reshape(pairs, 2)]
    pad x2 -> x0, local copies, waits for them, and re-layouts: 1.43 us -> none  [the longest x1 0.81 us: sweep(): jnp.pad(column_ops[0], ((0, 0), (0, rows - levels), (0, rows - levels)))]
    unnamed x0 -> x1, other arithmetic: none -> 0.85 us
    unnamed x16 -> x15, local copies, waits for them, and re-layouts: 2.54 us -> 2.07 us
where the time goes in v1:
time: 59.8 us; the launch traced here: 59.6 us
  Pallas kernels  52.7 us (88%)
  matrix products  3.58 us (6%)
  local copies, waits for them, and re-layouts  2.39 us (4%)
  other arithmetic  0.85 us (1%)
    pallas_call x1, Pallas kernels, sweep(): pl.pallas_call(functools.partial(sweep_kernel, levels, rows, group, lanes...  33.3 us
    pallas_call x1, Pallas kernels, exchange(): pl.pallas_call(functools.partial(exchange_kernel, tiles, cap), out_shape=...  19.4 us
    dot_general x1, matrix products, body(): jnp.dot(surf_read[0], adjoint_state[0], preferred_element_type=F32)  3.58 us
    unnamed x15, local copies, waits for them, and re-layouts  2.07 us

profile of v1, /device:TPU:0, one launch (start us, length us, event | category | flops | bytes accessed | tf_op | source)
XLA Modules:
  0.0 59.6 jit_solution(16236573428980291403)
XLA Ops:
  0.0 0.0 copy-start
  0.0 0.0 copy-start.4
  0.0 0.0 copy-start.3
  0.0 0.0 copy-start.2
  0.0 0.0 copy-start.1
  0.0 0.0 copy-start.5
  0.0 0.8 %reduce = s32[576]{0:T(1024)S(1)} reduce(s32[1,576]{1,0:T(1,128)} %param.19, s32[]{:T(128)} %constant.10), dimensions={0}, to_apply=%param.19.reduce_sub_computation | reduce | bytes 4612 | tf_op args[9]
  0.9 0.1 reshape.17
  1.0 0.1 copy.14
  1.1 0.1 reshape.18.owned_ref
  1.2 0.0 copy-done
  1.2 3.6 %fusion.1 = bf16[1,4,288,128]{3,1,2,0:T(4,128)(2,1)S(1)} fusion(bf16[1,75,36864]{2,1,0:T(8,128)(2,1)} %state_ref.1, bf16[1,4,75]{2,1,0:T(4,128)(2,1)S(1)} %copy-done), kind=kOutput, calls=%fused_computation.2 | convolution fusion | flops 22265856 | bytes 5825112 | tf_op jit(solution)/shard_map/dot_general | solution.py:341
  4.8 0.0 copy-done.4
  4.8 0.0 copy-done.3
  4.9 0.0 copy-done.2
  4.9 0.0 copy-done.1
  4.9 19.4 %exchange.1 = f32[4,288,128]{2,1,0:T(8,128)S(1)} custom-call(bf16[4,288,128]{2,1,0:T(8,128)(2,1)S(1)} %bitcast.29, bf16[256,4096]{1,0:T(8,128)(2,1)S(1)} %bitcast.28, s32[16,16]{1,0:T(8,128)S(1)} %bitcast.30, s32[16,16]{1,0:T(8,128)S(1)} %bitcast.31, s32[1,16]{1,0:T(1,128)S(1)} %copy-done.4, s32[1,576]{1,0:T(1,128)S(1)} %reshape.18.owned_ref), custom_call_target="tpu_custom_call" | custom-call | tf_op jit(solution)/shard_map/exchange/pallas_call | solution.py:212
  24.3 1.2 %copy.20 = f32[1,4,288,128]{3,1,2,0:T(4,128)} copy(f32[1,4,288,128]{3,2,1,0:T(8,128)S(1)} %bitcast.27) | data formatting | bytes 1179648
  25.5 0.0 copy-done.5
  25.5 0.8 %copy.21 = bf16[1,16,75,75]{3,2,1,0:T(8,128)(2,1)} copy(bf16[1,16,75,75]{3,1,2,0:T(8,128)(2,1)S(1)} %copy-done.5) | data formatting | bytes 360000 | tf_op args[2]
  26.3 33.3 %sweep.1 = bf16[1,75,36864]{2,1,0:T(8,128)(2,1)} custom-call(bf16[1,75,36864]{2,1,0:T(8,128)(2,1)} %state_ref.1, bf16[1,75,36864]{2,1,0:T(8,128)(2,1)} %coef_ref.1, bf16[16,75,75]{2,1,0:T(8,128)(2,1)} %bitcast.33, f32[4,75]{1,0:T(4,128)} %bitcast.35, f32[4,36864]{1,0:T(4,128)} %bitcast.32), custom_call_target="tpu_custom_call" | custom-call | tf_op jit(solution)/shard_map/sweep/pallas_call | solution.py:307
  (1 shorter events, 0.0 us)
Async XLA Ops:
  0.0 1.2 %copy-start = (bf16[1,4,75]{2,1,0:T(4,128)(2,1)S(1)}, bf16[1,4,75]{2,1,0:T(4,128)(2,1)}, u32[]{:S(2)}) copy-start(bf16[1,4,75]{2,1,0:T(4,128)(2,1)} %param.13) | copy-start | bytes 1804
  0.0 4.8 %copy-start.4 = (s32[1,16]{1,0:T(1,128)S(1)}, s32[1,16]{1,0:T(1,128)}, u32[]{:S(2)}) copy-start(s32[1,16]{1,0:T(1,128)} %len_ref.1) | copy-start | bytes 196
  0.0 4.8 %copy-start.3 = (s32[1,16,16]{2,1,0:T(8,128)S(1)}, s32[1,16,16]{2,1,0:T(8,128)}, u32[]{:S(2)}) copy-start(s32[1,16,16]{2,1,0:T(8,128)} %param.17) | copy-start | bytes 3076
  0.0 4.8 %copy-start.2 = (s32[1,16,16]{2,1,0:T(8,128)S(1)}, s32[1,16,16]{2,1,0:T(8,128)}, u32[]{:S(2)}) copy-start(s32[1,16,16]{2,1,0:T(8,128)} %param.16) | copy-start | bytes 3076
  0.0 4.9 %copy-start.1 = (bf16[1,16,16,4096]{3,2,1,0:T(8,128)(2,1)S(1)}, bf16[1,16,16,4096]{3,2,1,0:T(8,128)(2,1)}, u32[]{:S(2)}) copy-start(bf16[1,16,16,4096]{3,2,1,0:T(8,128)(2,1)} %param.15) | copy-start | bytes 6291460
  0.0 25.4 %copy-start.5 = (bf16[1,16,75,75]{3,1,2,0:T(8,128)(2,1)S(1)}, bf16[1,16,75,75]{3,1,2,0:T(8,128)(2,1)}, u32[]{:S(2)}) copy-start(bf16[1,16,75,75]{3,1,2,0:T(8,128)(2,1)} %param.12) | copy-start | bytes 540004

commit v2 on v1

v2 whole, which is shorter than its diff:
```python
import functools

import jax
import jax.numpy as jnp
from jax import lax
from jax.experimental import pallas as pl
from jax.experimental.pallas import tpu as pltpu
from jax.sharding import PartitionSpec as P

NF = 4
BLK = 64
MXU = 256
MESH = pl.DeviceIdType.MESH
F32 = jnp.float32
BF16 = jnp.bfloat16


def round_up(value, unit):
    return -(-value // unit) * unit


def iota(shape, axis):
    return lax.broadcasted_iota(jnp.int32, shape, axis)


def dot(left, right, contract=((1,), (0,))):
    return lax.dot_general(left, right, (contract, ((), ())), preferred_element_type=F32)


def one_hot(condition):
    return jnp.where(condition, 1.0, 0.0).astype(BF16)


def slot_column(rows, cap):
    spread = jnp.concatenate([jnp.broadcast_to(row, (cap, row.shape[1])) for row in rows], axis=0)
    chosen = iota(spread.shape, 1) == lax.rem(iota(spread.shape, 0), cap)
    return jnp.sum(jnp.where(chosen, spread.astype(F32), 0.0), axis=1, keepdims=True)


def build_operators(levels, rows, group, ops_ref, big):
    full = big.shape[1]
    lane = iota((rows, full), 1)
    target = iota((levels, full), 1)
    tiler = one_hot((lax.rem(target, rows) == iota((levels, full), 0)) & (target < group * rows))
    blank = jnp.zeros((rows - levels, levels), F32)
    for step in range(ops_ref.shape[0]):
        operator = jnp.concatenate([ops_ref[step].astype(F32), blank], axis=0).astype(BF16)
        tiled = dot(operator, tiler)
        for part in range(group):
            inside = (lane >= part * rows) & (lane < (part + 1) * rows)
            big[step, part * rows : (part + 1) * rows, :] = jnp.where(inside, tiled, 0.0).astype(BF16)
        if full > group * rows:
            big[step, group * rows :, :] = jnp.zeros((full - group * rows, full), BF16)


def stack_columns(pieces, full):
    stacked = sum(piece.shape[0] for piece in pieces)
    if full > stacked:
        pieces = pieces + [jnp.zeros((full - stacked, pieces[0].shape[1]), BF16)]
    return jnp.concatenate(pieces, axis=0).T


def all_steps(current, factors, big):
    for step in range(big.shape[0]):
        for unit in range(len(current)):
            current[unit] = (dot(current[unit], big[step]) * factors[unit]).astype(BF16)
    return current


def exchange_kernel(
    tiles, cap, levels, rows, group, lanes, units,
    surface_ref, weights_ref, atmos_ref, ocean_ref, len_ref, owned_ref, state_ref, coef_ref, ops_ref,
    out_ref, swept_ref,
    ids_send, ids_recv, flux_send, flux_recv, reply_send, reply_recv, back_half, back_recv, place_buf,
    expanded, summed, folded, state_buf, coef_buf, big, sems, load_sems,
):
    section = lax.axis_index("sec")
    me = lax.axis_index("tile")
    other = 1 - section
    slots = tiles * cap
    half = tiles // 2
    half_slots = half * cap
    pairs = surface_ref.shape[1]
    blocks = 2 * pairs
    wide = 2 * MXU
    chunks = weights_ref.shape[1] // wide
    per_chunk = wide // BLK
    ids_out, ids_in, flux_out, flux_in, reply_out, reply_in, back_out, back_in = [sems.at[i] for i in range(8)]

    def peer(i):
        return lax.rem(me + i, tiles)

    early = swept_ref.shape[0]
    block_cells = group * lanes * units
    full = big.shape[1]

    def load(source, target, kind, j):
        start = pl.multiple_of(j * block_cells, block_cells)
        return pltpu.make_async_copy(
            source.at[0, :, pl.ds(start, block_cells)], target.at[j], load_sems.at[kind, j]
        )

    for j in range(early):
        load(state_ref, state_buf, 0, j).start()
        load(coef_ref, coef_buf, 1, j).start()

    def sweep_blocks(first, last):
        @pl.loop(first, last)
        def _(j):
            load(state_ref, state_buf, 0, j).wait()
            load(coef_ref, coef_buf, 1, j).wait()

            def columns(unit, part):
                return pl.ds((unit * group + part) * lanes, lanes)

            def stacked(buffer, unit):
                pieces = []
                for part in range(group):
                    piece = buffer[j, :, columns(unit, part)].astype(F32)
                    blank = jnp.zeros((rows - levels, lanes), F32)
                    pieces.append(jnp.concatenate([piece, blank], axis=0).astype(BF16))
                return stack_columns(pieces, full)

            current = [stacked(state_buf, unit) for unit in range(units)]
            factors = [stacked(coef_buf, unit).astype(F32) for unit in range(units)]
            current = all_steps(current, factors, big)
            for unit in range(units):
                swept = current[unit].T
                for part in range(group):
                    swept_ref[j, :, columns(unit, part)] = swept[part * rows : (part + 1) * rows]

    barrier = pltpu.get_barrier_semaphore()

    @pl.loop(0, tiles)
    def _(i):
        pl.semaphore_signal(barrier, inc=1, device_id=(other, peer(i)), device_id_type=MESH)

    @pl.when(section == 1)
    def _():
        @pl.loop(1, tiles)
        def _(i):
            pl.semaphore_signal(barrier, inc=1, device_id=(section, peer(i)), device_id_type=MESH)

    def send(source, target, send_sem, recv_sem, first, to):
        @pl.loop(first, tiles)
        def _(i):
            pltpu.make_async_remote_copy(
                src_ref=source.at[peer(i)],
                dst_ref=target,
                send_sem=send_sem,
                recv_sem=recv_sem,
                device_id=(to, peer(i)),
                device_id_type=MESH,
            ).start()

    def wait_all(buffer, sem):
        pltpu.make_async_copy(buffer, buffer, sem).wait()

    def surface_rows():
        lower = [surface_ref[n, :, 0:BLK] for n in range(NF)]
        upper = [surface_ref[n, :, BLK : 2 * BLK] for n in range(NF)]
        return jnp.concatenate([jnp.concatenate(lower, axis=1), jnp.concatenate(upper, axis=1)], axis=0)

    def emit(forcing):
        for n in range(NF):
            lanes = slice(n * BLK, (n + 1) * BLK)
            out_ref[:, n, :] = jnp.concatenate([forcing[:pairs, lanes], forcing[pairs:, lanes]], axis=1)

    def weights_at(q, first, count):
        return weights_ref[first : first + count, pl.ds(pl.multiple_of(q * wide, wide), wide)].astype(F32)

    def back_terms(first):
        echoes = reply_recv[...].reshape(half_slots, MXU)
        for n in range(NF):
            repeat = one_hot(iota((MXU, MXU), 0) == n * BLK + lax.rem(iota((MXU, MXU), 1), BLK))
            expanded[n] = dot(echoes, repeat)
        folded[...] = jnp.zeros_like(folded)

        @pl.loop(0, chunks)
        def _(q):
            weights = weights_at(q, first, half_slots)
            gather = one_hot(iota((wide, BLK), 1) == q * per_chunk + iota((wide, BLK), 0) // BLK)
            for n in range(NF):
                copies = jnp.concatenate([expanded[n], expanded[n]], axis=1)
                folded[n] += dot((copies * weights).astype(BF16), gather)

        back_half[...] = jnp.concatenate([folded[n] for n in range(NF)], axis=1).astype(BF16)

    build_operators(levels, rows, group, ops_ref, big)

    @pl.when(section == 0)
    def _():
        for d in range(tiles):
            ids_send[d, 0:1, 0:cap] = ocean_ref[d : d + 1, :]
        source = slot_column([atmos_ref[d : d + 1, :] for d in range(tiles)], cap)
        spread = jnp.broadcast_to(len_ref[...], (slots, tiles))
        owner = iota((slots, tiles), 1) == iota((slots, tiles), 0) // cap
        length = jnp.sum(jnp.where(owner, spread.astype(F32), 0.0), axis=1, keepdims=True)
        live = lax.rem(iota((slots, 1), 0), cap).astype(F32) < length
        lane = iota((slots, blocks), 1)
        block = 2 * lax.rem(lane, pairs) + lane // pairs
        place = one_hot((block.astype(F32) == source) & live)
        place_buf[...] = place
        picked = dot(place, surface_rows()).astype(BF16)
        fields = [picked[:, n * BLK : (n + 1) * BLK] for n in range(NF)]
        summed[...] = jnp.zeros_like(summed)

        @pl.loop(0, chunks)
        def _(q):
            weights = weights_at(q, 0, slots)
            widen = one_hot(iota((BLK, wide), 0) == q * per_chunk + iota((BLK, wide), 1) // BLK)
            for n in range(NF):
                terms = dot(fields[n], widen) * weights
                summed[n] += terms[:, :MXU] + terms[:, MXU:]

        flux = jnp.zeros((slots, MXU), F32)
        for n in range(NF):
            fold = one_hot(iota((MXU, MXU), 1) == n * BLK + lax.rem(iota((MXU, MXU), 0), BLK))
            flux += dot(summed[n].astype(BF16), fold)
        flux_send[...] = flux.astype(BF16).reshape(tiles, cap, MXU)

    third = early // 3
    middle = third * (1 + section)
    sweep_blocks(0, middle)

    @pl.when(section == 0)
    def _():
        pl.semaphore_wait(barrier, tiles)
        send(ids_send, ids_recv.at[me], ids_out, ids_in, 0, 1)
        send(flux_send, flux_recv.at[me], flux_out, flux_in, 0, 1)

    @pl.when(section == 1)
    def _():
        pl.semaphore_wait(barrier, 2 * tiles - 1)
        surface = surface_rows()
        wait_all(ids_recv, ids_in)
        wanted = slot_column([ids_recv[t, 0:1, :] for t in range(tiles)], cap)
        place = one_hot(owned_ref[...].astype(F32) == wanted)
        place_buf[...] = place
        reply_send[...] = dot(place, surface).astype(BF16).reshape(tiles, cap, MXU)

        @pl.when(me >= half)
        def _():
            send(reply_send, reply_recv.at[me - half], reply_out, reply_in, 1, 1)
            reply_recv[me - half] = reply_send[me]

        @pl.when(me < half)
        def _():
            send(reply_send, reply_recv.at[me], reply_out, reply_in, 0, 0)

    sweep_blocks(middle, early)

    @pl.when(section == 0)
    def _():
        wait_all(reply_recv, reply_in)
        back_terms(0)
        wait_all(back_recv, back_in)
        back = jnp.concatenate([back_half[...], back_recv[...]], axis=0)
        emit(dot(place_buf[...], back, ((0,), (0,))))
        wait_all(ids_send, ids_out)
        wait_all(flux_send, flux_out)

    @pl.when(section == 1)
    def _():
        upper = me >= half

        @pl.when(upper)
        def _():
            wait_all(reply_recv.at[pl.ds(0, half - 1)], reply_in)

        @pl.when(jnp.logical_not(upper))
        def _():
            wait_all(reply_recv, reply_in)

        back_terms(half_slots)
        back_copy = pltpu.make_async_remote_copy(
            src_ref=back_half,
            dst_ref=back_recv,
            send_sem=back_out,
            recv_sem=back_in,
            device_id=(other, me),
            device_id_type=MESH,
        )
        back_copy.start()
        wait_all(flux_recv, flux_in)
        emit(dot(place_buf[...], flux_recv[...].reshape(slots, MXU), ((0,), (0,))))
        back_copy.wait_send()

        @pl.when(upper)
        def _():
            wait_all(reply_send.at[pl.ds(0, tiles - 1)], reply_out)

        @pl.when(jnp.logical_not(upper))
        def _():
            wait_all(reply_send, reply_out)


def layout(levels, cells):
    rows = round_up(levels, 16)
    full = round_up(rows, MXU)
    group = full // rows
    lanes = next(lanes for lanes in (512, 256, 128) if cells % (4 * group * lanes) == 0)
    return rows, full, group, lanes, 2


def exchange(surface, weights, pair_atmos, pair_ocean, list_len, owned, state, coef, operators):
    tiles, cap = pair_atmos.shape
    pairs = surface.shape[1]
    slots = tiles * cap
    half = tiles // 2
    _, levels, cells = state.shape
    steps = operators.shape[0]
    rows, full, group, lanes, units = layout(levels, cells)
    block = group * lanes * units
    early = cells // block // 2
    in_vmem = pl.BlockSpec(memory_space=pltpu.VMEM)
    in_place = pl.BlockSpec(memory_space=pl.ANY)
    return pl.pallas_call(
        functools.partial(exchange_kernel, tiles, cap, levels, rows, group, lanes, units),
        out_shape=(
            jax.ShapeDtypeStruct((pairs, NF, 2 * BLK), F32),
            jax.ShapeDtypeStruct((early, rows, block), BF16),
        ),
        in_specs=[in_vmem] * 6 + [in_place] * 2 + [in_vmem],
        out_specs=(in_vmem, in_vmem),
        scratch_shapes=[
            pltpu.VMEM((tiles, 8, 128), jnp.int32),
            pltpu.VMEM((tiles, 8, 128), jnp.int32),
            pltpu.VMEM((tiles, cap, MXU), BF16),
            pltpu.VMEM((tiles, cap, MXU), BF16),
            pltpu.VMEM((tiles, cap, MXU), BF16),
            pltpu.VMEM((half, cap, MXU), BF16),
            pltpu.VMEM((half * cap, MXU), BF16),
            pltpu.VMEM((half * cap, MXU), BF16),
            pltpu.VMEM((slots, 2 * pairs), BF16),
            pltpu.VMEM((NF, half * cap, MXU), F32),
            pltpu.VMEM((NF, slots, MXU), F32),
            pltpu.VMEM((NF, half * cap, BLK), F32),
            pltpu.VMEM((early, levels, block), BF16),
            pltpu.VMEM((early, levels, block), BF16),
            pltpu.VMEM((steps, full, full), BF16),
            pltpu.SemaphoreType.DMA((8,)),
            pltpu.SemaphoreType.DMA((2, early)),
        ],
        compiler_params=pltpu.CompilerParams(
            collective_id=0, has_side_effects=True, vmem_limit_bytes=56 * 1024 * 1024
        ),
        name="exchange",
    )(surface, weights, pair_atmos, pair_ocean, list_len, owned, state, coef, operators)


def sweep_kernel(
    levels, rows, group, lanes, units, early,
    state_ref, coef_ref, ops_ref, write_ref, forcing_ref, swept_ref, out_ref, big,
):
    index = pl.program_id(0)
    full = big.shape[1]

    @pl.when(index == 0)
    def _():
        build_operators(levels, rows, group, ops_ref, big)

    def columns(unit, part):
        return pl.ds((unit * group + part) * lanes, lanes)

    write = write_ref[:, 0:rows]
    write_high = write.astype(BF16).astype(F32)
    write_parts = jnp.concatenate([write_high, write_high, write - write_high], axis=0).astype(BF16)

    def finish(swept, unit, part):
        first = (unit * group + part) * lanes // (2 * BLK)
        forcing = jnp.concatenate([forcing_ref[first + r] for r in range(lanes // (2 * BLK))], axis=1)
        high = forcing.astype(BF16).astype(F32)
        parts = jnp.concatenate([high, forcing - high, high], axis=0).astype(BF16)
        added = dot(write_parts, parts, ((0,), (0,)))
        out_ref[0, :, columns(unit, part)] = (swept.astype(F32) + added).astype(BF16)

    @pl.when(index < early)
    def _():
        half = units // 2
        for unit in range(units):
            for part in range(group):
                finish(swept_ref[unit // half, :, columns(unit % half, part)], unit, part)

    @pl.when(index >= early)
    def _():
        valid = iota((rows, lanes), 0) < levels

        def stacked(ref, unit):
            pieces = [
                jnp.where(valid, ref[0, :, columns(unit, part)].astype(F32), 0.0).astype(BF16)
                for part in range(group)
            ]
            return stack_columns(pieces, full)

        current = [stacked(state_ref, unit) for unit in range(units)]
        factors = [stacked(coef_ref, unit).astype(F32) for unit in range(units)]
        current = all_steps(current, factors, big)
        for unit in range(units):
            swept = current[unit].T
            for part in range(group):
                finish(swept[part * rows : (part + 1) * rows], unit, part)


def sweep(state, coef, operators, surf_write, forcing, swept):
    _, levels, cells = state.shape
    steps = operators.shape[0]
    rows, full, group, lanes, units = layout(levels, cells)
    units = 2 * units
    block = group * lanes * units
    early = swept.shape[0] // 2
    wide = pl.BlockSpec((1, rows, block), lambda i: (0, 0, jnp.maximum(i, early)))
    return pl.pallas_call(
        functools.partial(sweep_kernel, levels, rows, group, lanes, units, early),
        out_shape=jax.ShapeDtypeStruct(state.shape, BF16),
        grid=(cells // block,),
        in_specs=[
            wide,
            wide,
            pl.BlockSpec(operators.shape, lambda i: (0, 0, 0)),
            pl.BlockSpec((NF, round_up(rows, 128)), lambda i: (0, 0)),
            pl.BlockSpec((block // (2 * BLK), NF, 2 * BLK), lambda i: (i, 0, 0)),
            pl.BlockSpec((2, rows, block // 2), lambda i: (jnp.minimum(i, early - 1), 0, 0)),
        ],
        out_specs=pl.BlockSpec((1, rows, block), lambda i: (0, 0, i)),
        scratch_shapes=[pltpu.VMEM((steps, full, full), BF16)],
        compiler_params=pltpu.CompilerParams(
            dimension_semantics=("arbitrary",), vmem_limit_bytes=56 * 1024 * 1024
        ),
        name="sweep",
    )(state, coef, operators, surf_write[0].T, forcing, swept)


def body(
    adjoint_state,
    tangent_coef,
    column_ops,
    surf_read,
    surf_write,
    remap_weights,
    pair_atmos,
    pair_ocean,
    list_len,
    ocean_owned,
):
    tiles, cap = pair_atmos.shape[1:]
    pairs = ocean_owned.shape[1] // 2
    surface = jnp.dot(surf_read[0], adjoint_state[0], preferred_element_type=F32).astype(BF16)
    owned = jnp.swapaxes(ocean_owned.reshape(pairs, 2), 0, 1).reshape(1, 2 * pairs)
    forcing, swept = exchange(
        surface.reshape(NF, pairs, 2 * BLK),
        remap_weights.reshape(tiles * cap, BLK * BLK),
        pair_atmos[0],
        pair_ocean[0],
        list_len,
        owned,
        adjoint_state,
        tangent_coef,
        column_ops[0],
    )
    return sweep(adjoint_state, tangent_coef, column_ops[0], surf_write, forcing, swept)


def solution(mesh):
    in_specs = (
        P("sec", None, "tile"),
        P("sec", None, "tile"),
        P("sec", None, None, None),
        P("sec", None, None),
        P("sec", None, None),
        P("tile", None, None, None),
        P("tile", None, None),
        P("tile", None, None),
        P("tile", None),
        P("tile", None),
    )
    out_specs = P("sec", None, "tile")
    return jax.shard_map(body, mesh=mesh, in_specs=in_specs, out_specs=out_specs, check_vma=False)
```

time: 59.8 us -> 60.3 us (level)
    pallas_call x1, Pallas kernels: 19.4 us -> 31.9 us  [exchange(): pl.pallas_call(functools.partial(exchange_kernel, tiles, cap, levels, row...]
    pallas_call x1, Pallas kernels: 33.3 us -> 21.3 us  [sweep(): pl.pallas_call(functools.partial(sweep_kernel, levels, rows, group, lanes...]
    reshape x1, local copies, waits for them, and re-layouts: 0.09 us -> 0.7 us  [body(): jnp.swapaxes(ocean_owned.reshape(pairs, 2), 0, 1).reshape(1, 2 * pairs)]
    unnamed x15 -> x6, local copies, waits for them, and re-layouts: 2.07 us -> 1.58 us
where the time goes in v2:
time: 60.3 us; the launch traced here: 60 us
  Pallas kernels  53.2 us (88%)
  matrix products  3.55 us (6%)
  local copies, waits for them, and re-layouts  2.5 us (4%)
  other arithmetic  0.74 us (1%)
    pallas_call x1, Pallas kernels, exchange(): pl.pallas_call(functools.partial(exchange_kernel, tiles, cap, levels, row...  31.9 us
    pallas_call x1, Pallas kernels, sweep(): pl.pallas_call(functools.partial(sweep_kernel, levels, rows, group, lanes...  21.3 us
    dot_general x1, matrix products, body(): jnp.dot(surf_read[0], adjoint_state[0], preferred_element_type=F32)  3.55 us
    unnamed x6, local copies, waits for them, and re-layouts  1.58 us

profile of v2, /device:TPU:0, one launch (start us, length us, event | category | flops | bytes accessed | tf_op | source)
XLA Modules:
  0.0 60.0 jit_solution(10507603090982278896)
XLA Ops:
  0.0 0.0 copy-start
  0.0 0.0 copy-start.1
  0.0 0.7 %reduce = s32[576]{0:T(1024)S(1)} reduce(s32[1,576]{1,0:T(1,128)} %param.19, s32[]{:T(128)} %constant.10), dimensions={0}, to_apply=%param.19.reduce_sub_computation | reduce | bytes 4612 | tf_op args[9]
  0.8 0.1 reshape.14
  0.9 0.1 copy.14
  1.0 0.7 %reshape.15.owned_ref = s32[1,576]{1,0:T(1,128)} reshape(s32[2,288]{1,0:T(2,128)S(1)} %copy.14) | data formatting | bytes 4608 | tf_op jit(solution)/shard_map/reshape | solution.py:449
  1.7 0.0 copy-done
  1.7 3.5 %fusion.1 = bf16[1,4,288,128]{3,1,2,0:T(4,128)(2,1)S(1)} fusion(bf16[1,75,36864]{2,1,0:T(8,128)(2,1)} %state_ref.3, bf16[1,4,75]{2,1,0:T(4,128)(2,1)S(1)} %copy-done), kind=kOutput, calls=%fused_computation.2 | convolution fusion | flops 22265856 | bytes 5825112 | tf_op jit(solution)/shard_map/dot_general | solution.py:448
  5.2 0.8 %copy.19 = bf16[1,4,288,128]{3,2,1,0:T(8,128)(2,1)} copy(bf16[1,4,288,128]{3,1,2,0:T(4,128)(2,1)S(1)} %fusion.1) | data formatting | bytes 589824
  6.0 0.0 copy-done.1
  6.0 0.8 %copy.18 = bf16[1,16,75,75]{3,2,1,0:T(8,128)(2,1)} copy(bf16[1,16,75,75]{3,1,2,0:T(8,128)(2,1)S(1)} %copy-done.1) | data formatting | bytes 360000 | tf_op args[2]
  6.8 31.9 %exchange.1 = (f32[288,4,128]{2,1,0:T(4,128)}, bf16[6,80,3072]{2,1,0:T(8,128)(2,1)}) custom-call(bf16[4,288,128]{2,1,0:T(8,128)(2,1)} %bitcast.26, bf16[256,4096]{1,0:T(8,128)(2,1)} %bitcast.25, s32[16,16]{1,0:T(8,128)} %bitcast.28, s32[16,16]{1,0:T(8,128)} %bitcast.29, s32[1,16]{1,0:T(1,128)} %len_ref.1, s32[1,576]{1,0:T(1,128)} %reshape.15.owned_ref, ...), custom_call_target="tpu_custom_call" | custom-call | tf_op jit(solution)/shard_map/exchange/pallas_call | solution.py:318
  38.8 21.3 %sweep.1 = bf16[1,75,36864]{2,1,0:T(8,128)(2,1)} custom-call(bf16[1,75,36864]{2,1,0:T(8,128)(2,1)} %state_ref.3, bf16[1,75,36864]{2,1,0:T(8,128)(2,1)} %coef_ref.3, bf16[16,75,75]{2,1,0:T(8,128)(2,1)} %bitcast.24, f32[4,75]{1,0:T(4,128)} %bitcast.30, f32[288,4,128]{2,1,0:T(4,128)} %get-tuple-element.7.forcing_ref, ...), custom_call_target="tpu_custom_call" | custom-call | tf_op jit(solution)/shard_map/sweep/pallas_call | solution.py:413
Async XLA Ops:
  0.0 1.7 %copy-start = (bf16[1,4,75]{2,1,0:T(4,128)(2,1)S(1)}, bf16[1,4,75]{2,1,0:T(4,128)(2,1)}, u32[]{:S(2)}) copy-start(bf16[1,4,75]{2,1,0:T(4,128)(2,1)} %param.13) | copy-start | bytes 1804
  0.0 6.0 %copy-start.1 = (bf16[1,16,75,75]{3,1,2,0:T(8,128)(2,1)S(1)}, bf16[1,16,75,75]{3,1,2,0:T(8,128)(2,1)}, u32[]{:S(2)}) copy-start(bf16[1,16,75,75]{3,1,2,0:T(8,128)(2,1)} %param.12) | copy-start | bytes 540004

commit v3 on v2

--- a/solution.py
+++ b/solution.py
@@ -125,9 +125,7 @@
             factors = [stacked(coef_buf, unit).astype(F32) for unit in range(units)]
             current = all_steps(current, factors, big)
             for unit in range(units):
-                swept = current[unit].T
-                for part in range(group):
-                    swept_ref[j, :, columns(unit, part)] = swept[part * rows : (part + 1) * rows]
+                swept_ref[j, unit * lanes : (unit + 1) * lanes, :] = current[unit]
 
     barrier = pltpu.get_barrier_semaphore()
 
@@ -180,11 +178,14 @@
         def _(q):
             weights = weights_at(q, first, half_slots)
             gather = one_hot(iota((wide, BLK), 1) == q * per_chunk + iota((wide, BLK), 0) // BLK)
+            products = []
             for n in range(NF):
                 copies = jnp.concatenate([expanded[n], expanded[n]], axis=1)
-                folded[n] += dot((copies * weights).astype(BF16), gather)
-
-        back_half[...] = jnp.concatenate([folded[n] for n in range(NF)], axis=1).astype(BF16)
+                products.append((copies * weights).astype(BF16))
+            folded[...] += dot(jnp.concatenate(products, axis=0), gather)
+
+        fields = [folded[n * half_slots : (n + 1) * half_slots] for n in range(NF)]
+        back_half[...] = jnp.concatenate(fields, axis=1).astype(BF16)
 
     build_operators(levels, rows, group, ops_ref, big)
 
@@ -202,15 +203,16 @@
         place = one_hot((block.astype(F32) == source) & live)
         place_buf[...] = place
         picked = dot(place, surface_rows()).astype(BF16)
-        fields = [picked[:, n * BLK : (n + 1) * BLK] for n in range(NF)]
+        fields = jnp.concatenate([picked[:, n * BLK : (n + 1) * BLK] for n in range(NF)], axis=0)
         summed[...] = jnp.zeros_like(summed)
 
         @pl.loop(0, chunks)
         def _(q):
             weights = weights_at(q, 0, slots)
             widen = one_hot(iota((BLK, wide), 0) == q * per_chunk + iota((BLK, wide), 1) // BLK)
+            widened = dot(fields, widen)
             for n in range(NF):
-                terms = dot(fields[n], widen) * weights
+                terms = widened[n * slots : (n + 1) * slots] * weights
                 summed[n] += terms[:, :MXU] + terms[:, MXU:]
 
         flux = jnp.zeros((slots, MXU), F32)
@@ -219,8 +221,7 @@
             flux += dot(summed[n].astype(BF16), fold)
         flux_send[...] = flux.astype(BF16).reshape(tiles, cap, MXU)
 
-    third = early // 3
-    middle = third * (1 + section)
+    middle = section * (2 * early // 3)
     sweep_blocks(0, middle)
 
     @pl.when(section == 0)
@@ -319,7 +320,7 @@
         functools.partial(exchange_kernel, tiles, cap, levels, rows, group, lanes, units),
         out_shape=(
             jax.ShapeDtypeStruct((pairs, NF, 2 * BLK), F32),
-            jax.ShapeDtypeStruct((early, rows, block), BF16),
+            jax.ShapeDtypeStruct((early, units * lanes, full), BF16),
         ),
         in_specs=[in_vmem] * 6 + [in_place] * 2 + [in_vmem],
         out_specs=(in_vmem, in_vmem),
@@ -335,7 +336,7 @@
             pltpu.VMEM((slots, 2 * pairs), BF16),
             pltpu.VMEM((NF, half * cap, MXU), F32),
             pltpu.VMEM((NF, slots, MXU), F32),
-            pltpu.VMEM((NF, half * cap, BLK), F32),
+            pltpu.VMEM((NF * half * cap, BLK), F32),
             pltpu.VMEM((early, levels, block), BF16),
             pltpu.VMEM((early, levels, block), BF16),
             pltpu.VMEM((steps, full, full), BF16),
@@ -351,36 +352,49 @@
 
 def sweep_kernel(
     levels, rows, group, lanes, units, early,
-    state_ref, coef_ref, ops_ref, write_ref, forcing_ref, swept_ref, out_ref, big,
+    state_ref, coef_ref, ops_ref, write_ref, forcing_ref, swept_ref, out_ref, big, write_big,
 ):
     index = pl.program_id(0)
     full = big.shape[1]
+    depth = write_big.shape[0]
+    strip = 4 * NF
 
     @pl.when(index == 0)
     def _():
         build_operators(levels, rows, group, ops_ref, big)
+        write = write_ref[:, 0:levels]
+        high = write.astype(BF16).astype(F32)
+        parts = jnp.concatenate([high, high, write - high, jnp.zeros_like(write)], axis=0).astype(BF16)
+        target = iota((levels, full), 1)
+        tiler = one_hot((lax.rem(target, rows) == iota((levels, full), 0)) & (target < group * rows))
+        tiled = dot(parts, tiler)
+        lane = iota((strip, full), 1)
+        write_big[...] = jnp.zeros_like(write_big)
+        for part in range(group):
+            inside = (lane >= part * rows) & (lane < (part + 1) * rows)
+            write_big[part * strip : (part + 1) * strip, :] = jnp.where(inside, tiled, 0.0).astype(BF16)
 
     def columns(unit, part):
         return pl.ds((unit * group + part) * lanes, lanes)
 
-    write = write_ref[:, 0:rows]
-    write_high = write.astype(BF16).astype(F32)
-    write_parts = jnp.concatenate([write_high, write_high, write - write_high], axis=0).astype(BF16)
-
-    def finish(swept, unit, part):
-        first = (unit * group + part) * lanes // (2 * BLK)
-        forcing = jnp.concatenate([forcing_ref[first + r] for r in range(lanes // (2 * BLK))], axis=1)
-        high = forcing.astype(BF16).astype(F32)
-        parts = jnp.concatenate([high, forcing - high, high], axis=0).astype(BF16)
-        added = dot(write_parts, parts, ((0,), (0,)))
-        out_ref[0, :, columns(unit, part)] = (swept.astype(F32) + added).astype(BF16)
+    def finish(swept, unit):
+        pieces = []
+        for part in range(group):
+            first = (unit * group + part) * lanes // (2 * BLK)
+            forcing = jnp.concatenate([forcing_ref[first + r] for r in range(lanes // (2 * BLK))], axis=1)
+            high = forcing.astype(BF16).astype(F32)
+            pieces.append(jnp.concatenate([high, forcing - high, high, jnp.zeros_like(high)], axis=0).astype(BF16))
+        added = dot(stack_columns(pieces, depth), write_big[...])
+        result = (swept.astype(F32) + added).astype(BF16).T
+        for part in range(group):
+            out_ref[0, :, columns(unit, part)] = result[part * rows : (part + 1) * rows]
 
     @pl.when(index < early)
     def _():
         half = units // 2
         for unit in range(units):
-            for part in range(group):
-                finish(swept_ref[unit // half, :, columns(unit % half, part)], unit, part)
+            first = unit % half * lanes
+            finish(swept_ref[unit // half, first : first + lanes, :], unit)
 
     @pl.when(index >= early)
     def _():
@@ -397,9 +411,7 @@
         factors = [stacked(coef_ref, unit).astype(F32) for unit in range(units)]
         current = all_steps(current, factors, big)
         for unit in range(units):
-            swept = current[unit].T
-            for part in range(group):
-                finish(swept[part * rows : (part + 1) * rows], unit, part)
+            finish(current[unit], unit)
 
 
 def sweep(state, coef, operators, surf_write, forcing, swept):
@@ -420,10 +432,13 @@
             pl.BlockSpec(operators.shape, lambda i: (0, 0, 0)),
             pl.BlockSpec((NF, round_up(rows, 128)), lambda i: (0, 0)),
             pl.BlockSpec((block // (2 * BLK), NF, 2 * BLK), lambda i: (i, 0, 0)),
-            pl.BlockSpec((2, rows, block // 2), lambda i: (jnp.minimum(i, early - 1), 0, 0)),
+            pl.BlockSpec((2, units // 2 * lanes, full), lambda i: (jnp.minimum(i, early - 1), 0, 0)),
         ],
         out_specs=pl.BlockSpec((1, rows, block), lambda i: (0, 0, i)),
-        scratch_shapes=[pltpu.VMEM((steps, full, full), BF16)],
+        scratch_shapes=[
+            pltpu.VMEM((steps, full, full), BF16),
+            pltpu.VMEM((round_up(4 * NF * group, 128), full), BF16),
+        ],
         compiler_params=pltpu.CompilerParams(
             dimension_semantics=("arbitrary",), vmem_limit_bytes=56 * 1024 * 1024
         ),

time: 60.3 us -> 57.3 us (0.950)
  Pallas kernels: 53.2 us -> 50.3 us
    pallas_call x1, Pallas kernels: 31.9 us -> 28.5 us  [exchange(): pl.pallas_call(functools.partial(exchange_kernel, tiles, cap, levels, row...]
where the time goes in v3:
time: 57.3 us; the launch traced here: 57.1 us
  Pallas kernels  50.3 us (88%)
  matrix products  3.55 us (6%)
  local copies, waits for them, and re-layouts  2.47 us (4%)
  other arithmetic  0.74 us (1%)
    pallas_call x1, Pallas kernels, exchange(): pl.pallas_call(functools.partial(exchange_kernel, tiles, cap, levels, row...  28.5 us
    pallas_call x1, Pallas kernels, sweep(): pl.pallas_call(functools.partial(sweep_kernel, levels, rows, group, lanes...  21.8 us
    dot_general x1, matrix products, body(): jnp.dot(surf_read[0], adjoint_state[0], preferred_element_type=F32)  3.55 us
    unnamed x6, local copies, waits for them, and re-layouts  1.56 us

profile of v3, /device:TPU:0, one launch (start us, length us, event | category | flops | bytes accessed | tf_op | source)
XLA Modules:
  0.0 57.1 jit_solution(855501071446252417)
XLA Ops:
  0.0 0.0 copy-start
  0.0 0.0 copy-start.1
  0.0 0.7 %reduce = s32[576]{0:T(1024)S(1)} reduce(s32[1,576]{1,0:T(1,128)} %param.19, s32[]{:T(128)} %constant.10), dimensions={0}, to_apply=%param.19.reduce_sub_computation | reduce | bytes 4612 | tf_op args[9]
  0.8 0.1 reshape.14
  0.9 0.1 copy.14
  1.0 0.7 %reshape.15.owned_ref = s32[1,576]{1,0:T(1,128)} reshape(s32[2,288]{1,0:T(2,128)S(1)} %copy.14) | data formatting | bytes 4608 | tf_op jit(solution)/shard_map/reshape | solution.py:464
  1.7 0.0 copy-done
  1.7 3.5 %fusion.1 = bf16[1,4,288,128]{3,1,2,0:T(4,128)(2,1)S(1)} fusion(bf16[1,75,36864]{2,1,0:T(8,128)(2,1)} %state_ref.3, bf16[1,4,75]{2,1,0:T(4,128)(2,1)S(1)} %copy-done), kind=kOutput, calls=%fused_computation.2 | convolution fusion | flops 22265856 | bytes 5825112 | tf_op jit(solution)/shard_map/dot_general | solution.py:463
  5.2 0.8 %copy.19 = bf16[1,4,288,128]{3,2,1,0:T(8,128)(2,1)} copy(bf16[1,4,288,128]{3,1,2,0:T(4,128)(2,1)S(1)} %fusion.1) | data formatting | bytes 589824
  6.0 0.0 copy-done.1
  6.0 0.8 %copy.18 = bf16[1,16,75,75]{3,2,1,0:T(8,128)(2,1)} copy(bf16[1,16,75,75]{3,1,2,0:T(8,128)(2,1)S(1)} %copy-done.1) | data formatting | bytes 360000 | tf_op args[2]
  6.8 28.5 %exchange.1 = (f32[288,4,128]{2,1,0:T(4,128)}, bf16[6,1024,256]{2,1,0:T(8,128)(2,1)}) custom-call(bf16[4,288,128]{2,1,0:T(8,128)(2,1)} %bitcast.26, bf16[256,4096]{1,0:T(8,128)(2,1)} %bitcast.25, s32[16,16]{1,0:T(8,128)} %bitcast.28, s32[16,16]{1,0:T(8,128)} %bitcast.29, s32[1,16]{1,0:T(1,128)} %len_ref.1, s32[1,576]{1,0:T(1,128)} %reshape.15.owned_ref, ...), custom_call_target="tpu_custom_call" | custom-call | tf_op jit(solution)/shard_map/exchange/pallas_call | solution.py:319
  35.3 21.8 %sweep.1 = bf16[1,75,36864]{2,1,0:T(8,128)(2,1)} custom-call(bf16[1,75,36864]{2,1,0:T(8,128)(2,1)} %state_ref.3, bf16[1,75,36864]{2,1,0:T(8,128)(2,1)} %coef_ref.3, bf16[16,75,75]{2,1,0:T(8,128)(2,1)} %bitcast.24, f32[4,75]{1,0:T(4,128)} %bitcast.30, f32[288,4,128]{2,1,0:T(4,128)} %get-tuple-element.7.forcing_ref, ...), custom_call_target="tpu_custom_call" | custom-call | tf_op jit(solution)/shard_map/sweep/pallas_call | solution.py:425
Async XLA Ops:
  0.0 1.7 %copy-start = (bf16[1,4,75]{2,1,0:T(4,128)(2,1)S(1)}, bf16[1,4,75]{2,1,0:T(4,128)(2,1)}, u32[]{:S(2)}) copy-start(bf16[1,4,75]{2,1,0:T(4,128)(2,1)} %param.13) | copy-start | bytes 1804
  0.0 6.0 %copy-start.1 = (bf16[1,16,75,75]{3,1,2,0:T(8,128)(2,1)S(1)}, bf16[1,16,75,75]{3,1,2,0:T(8,128)(2,1)}, u32[]{:S(2)}) copy-start(bf16[1,16,75,75]{3,1,2,0:T(8,128)(2,1)} %param.12) | copy-start | bytes 540004

commit v4 on v3

--- a/solution.py
+++ b/solution.py
@@ -43,9 +43,13 @@
     target = iota((levels, full), 1)
     tiler = one_hot((lax.rem(target, rows) == iota((levels, full), 0)) & (target < group * rows))
     blank = jnp.zeros((rows - levels, levels), F32)
-    for step in range(ops_ref.shape[0]):
-        operator = jnp.concatenate([ops_ref[step].astype(F32), blank], axis=0).astype(BF16)
-        tiled = dot(operator, tiler)
+    steps = ops_ref.shape[0]
+    pieces = []
+    for step in range(steps):
+        pieces.append(jnp.concatenate([ops_ref[step].astype(F32), blank], axis=0).astype(BF16))
+    all_tiled = dot(jnp.concatenate(pieces, axis=0), tiler).astype(BF16)
+    for step in range(steps):
+        tiled = all_tiled[step * rows : (step + 1) * rows].astype(F32)
         for part in range(group):
             inside = (lane >= part * rows) & (lane < (part + 1) * rows)
             big[step, part * rows : (part + 1) * rows, :] = jnp.where(inside, tiled, 0.0).astype(BF16)

time: 57.3 us -> 57.3 us (level)
  no operation moved by 1% of the time
where the time goes in v4:
time: 57.3 us; the launch traced here: 57.1 us
  Pallas kernels  50.3 us (88%)
  matrix products  3.55 us (6%)
  local copies, waits for them, and re-layouts  2.47 us (4%)
  other arithmetic  0.74 us (1%)
    pallas_call x1, Pallas kernels, exchange(): pl.pallas_call(functools.partial(exchange_kernel, tiles, cap, levels, row...  28.5 us
    pallas_call x1, Pallas kernels, sweep(): pl.pallas_call(functools.partial(sweep_kernel, levels, rows, group, lanes...  21.8 us
    dot_general x1, matrix products, body(): jnp.dot(surf_read[0], adjoint_state[0], preferred_element_type=F32)  3.55 us
    unnamed x6, local copies, waits for them, and re-layouts  1.56 us

profile of v4, /device:TPU:0, one launch (start us, length us, event | category | flops | bytes accessed | tf_op | source)
XLA Modules:
  0.0 57.1 jit_solution(8293660312503771813)
XLA Ops:
  0.0 0.0 copy-start
  0.0 0.0 copy-start.1
  0.0 0.7 %reduce = s32[576]{0:T(1024)S(1)} reduce(s32[1,576]{1,0:T(1,128)} %param.19, s32[]{:T(128)} %constant.10), dimensions={0}, to_apply=%param.19.reduce_sub_computation | reduce | bytes 4612 | tf_op args[9]
  0.8 0.1 reshape.14
  0.9 0.1 copy.14
  1.0 0.7 %reshape.15.owned_ref = s32[1,576]{1,0:T(1,128)} reshape(s32[2,288]{1,0:T(2,128)S(1)} %copy.14) | data formatting | bytes 4608 | tf_op jit(solution)/shard_map/reshape | solution.py:468
  1.7 0.0 copy-done
  1.7 3.5 %fusion.1 = bf16[1,4,288,128]{3,1,2,0:T(4,128)(2,1)S(1)} fusion(bf16[1,75,36864]{2,1,0:T(8,128)(2,1)} %state_ref.3, bf16[1,4,75]{2,1,0:T(4,128)(2,1)S(1)} %copy-done), kind=kOutput, calls=%fused_computation.2 | convolution fusion | flops 22265856 | bytes 5825112 | tf_op jit(solution)/shard_map/dot_general | solution.py:467
  5.2 0.8 %copy.19 = bf16[1,4,288,128]{3,2,1,0:T(8,128)(2,1)} copy(bf16[1,4,288,128]{3,1,2,0:T(4,128)(2,1)S(1)} %fusion.1) | data formatting | bytes 589824
  6.0 0.0 copy-done.1
  6.0 0.8 %copy.18 = bf16[1,16,75,75]{3,2,1,0:T(8,128)(2,1)} copy(bf16[1,16,75,75]{3,1,2,0:T(8,128)(2,1)S(1)} %copy-done.1) | data formatting | bytes 360000 | tf_op args[2]
  6.8 28.5 %exchange.1 = (f32[288,4,128]{2,1,0:T(4,128)}, bf16[6,1024,256]{2,1,0:T(8,128)(2,1)}) custom-call(bf16[4,288,128]{2,1,0:T(8,128)(2,1)} %bitcast.26, bf16[256,4096]{1,0:T(8,128)(2,1)} %bitcast.25, s32[16,16]{1,0:T(8,128)} %bitcast.28, s32[16,16]{1,0:T(8,128)} %bitcast.29, s32[1,16]{1,0:T(1,128)} %len_ref.1, s32[1,576]{1,0:T(1,128)} %reshape.15.owned_ref, ...), custom_call_target="tpu_custom_call" | custom-call | tf_op jit(solution)/shard_map/exchange/pallas_call | solution.py:323
  35.3 21.8 %sweep.1 = bf16[1,75,36864]{2,1,0:T(8,128)(2,1)} custom-call(bf16[1,75,36864]{2,1,0:T(8,128)(2,1)} %state_ref.3, bf16[1,75,36864]{2,1,0:T(8,128)(2,1)} %coef_ref.3, bf16[16,75,75]{2,1,0:T(8,128)(2,1)} %bitcast.24, f32[4,75]{1,0:T(4,128)} %bitcast.30, f32[288,4,128]{2,1,0:T(4,128)} %get-tuple-element.7.forcing_ref, ...), custom_call_target="tpu_custom_call" | custom-call | tf_op jit(solution)/shard_map/sweep/pallas_call | solution.py:429
Async XLA Ops:
  0.0 1.7 %copy-start = (bf16[1,4,75]{2,1,0:T(4,128)(2,1)S(1)}, bf16[1,4,75]{2,1,0:T(4,128)(2,1)}, u32[]{:S(2)}) copy-start(bf16[1,4,75]{2,1,0:T(4,128)(2,1)} %param.13) | copy-start | bytes 1804
  0.0 6.0 %copy-start.1 = (bf16[1,16,75,75]{3,1,2,0:T(8,128)(2,1)S(1)}, bf16[1,16,75,75]{3,1,2,0:T(8,128)(2,1)}, u32[]{:S(2)}) copy-start(bf16[1,16,75,75]{3,1,2,0:T(8,128)(2,1)} %param.12) | copy-start | bytes 540004
